TPU v7x, 768 devices: a whole 4x8x12 slice. The times are simulated.
768 devices in a mesh: dp: 16 (over y, core), expert: 48 (over z, x).
Axes of the slice: x: 4, y: 8, z: 12, core: 2. Of those that a mesh axis runs over, the one named last changes fastest.
Arguments:
- tokens: bfloat16 [12288, 7168], P('expert', 'dp'), may hold values from -6 to 6
- cotangent: bfloat16 [12288, 7168], P('expert', 'dp'), may hold values from -1.796875 to 1.796875
- expert_ids: int32 [12288, 8], P('expert'), may hold values from 0 to 255, as said below
- route_probs: bfloat16 [12288, 8], P('expert'), may hold values from 0.099609375 to 1
- w_up: bfloat16 [48, 7168, 1024], P('expert', 'dp'), may hold values from -0.0625 to 0.0625
- w_down: bfloat16 [48, 1024, 7168], P('expert', None, 'dp'), may hold values from -0.1875 to 0.1875
Outputs:
- grad_tokens: bfloat16 [12288, 7168], P('expert', 'dp')
- grad_probs: bfloat16 [12288, 8], P('expert')
- grad_up: bfloat16 [48, 7168, 1024], P('expert', 'dp')
- grad_down: bfloat16 [48, 1024, 7168], P('expert', None, 'dp')
Inputs may be any that keep to these rules, and one draw needn't show every extreme that they name: `expert_ids`: A token names each id at most once. Within one block of 256 tokens each id below 48 is named by at most 8 tokens; one such id is named by exactly 8 tokens in every block, and in most blocks another one too; loads of the ids below 48 are strongly uneven.
All inputs are finite; a program needn't handle non-finite values.
Results may differ from a plain program's by a relative error of at most 0.008.
Values may be sent and summed in bfloat16 or wider, within the bound.
A program may use at most 32 MiB of HBM per device.

v0:
```python
import jax
import jax.numpy as jnp
from jax import lax
from jax.sharding import PartitionSpec as P

CAP = 8


def activate(hidden, query, gate_rows):
    sigma_h = jax.nn.sigmoid(hidden)
    act_rows = (hidden * sigma_h).astype(jnp.bfloat16)
    score_rows = jnp.sum(act_rows.astype(jnp.float32) * query, axis=1).astype(jnp.bfloat16)
    hidden_grad = (gate_rows[:, None] * query * sigma_h * (1.0 + hidden * (1.0 - sigma_h))).astype(
        jnp.bfloat16
    )
    return (act_rows, hidden_grad, score_rows)


def contract(left, right, left_dim, right_dim):
    return lax.dot_general(
        left, right, (((left_dim,), (right_dim,)), ((), ())), preferred_element_type=jnp.float32
    )


def on_device(tokens, cotangent, expert_ids, route_probs, w_up, w_down):
    experts = lax.axis_size("expert")
    block_rows = tokens.shape[0]
    feat_width = tokens.shape[1]
    top_count = expert_ids.shape[1]
    slot_count = experts * CAP
    numbers = jnp.arange(experts, dtype=jnp.int32)
    chosen = (expert_ids[:, :, None] == numbers[None, None, :]).astype(jnp.int32)
    per_token = jnp.sum(chosen, axis=1)
    before = jnp.cumsum(per_token, axis=0) - per_token
    order_rank = jnp.sum(chosen * before[:, None, :], axis=2)
    target = jnp.where(expert_ids < experts, expert_ids * CAP + order_rank, slot_count)
    placed = (target[:, :, None] == jnp.arange(slot_count, dtype=jnp.int32)[None, None, :]).astype(
        jnp.bfloat16
    )
    holder = jnp.sum(placed, axis=1)
    flat_placed = placed.reshape(block_rows * top_count, slot_count)
    stacked = jnp.concatenate([tokens, cotangent], axis=1)
    outgoing = contract(holder, stacked, 0, 0).astype(jnp.bfloat16)
    weights_out = contract(flat_placed, route_probs.reshape(-1), 0, 0).astype(jnp.bfloat16)
    send_x = outgoing[:, :feat_width].reshape(experts, CAP, feat_width)
    send_dy = outgoing[:, feat_width:].reshape(experts, CAP, feat_width)
    send_gate = weights_out.reshape(experts, CAP)
    rows_x, rows_dy, rows_gate = (
        lax.all_to_all(send_x, "expert", split_axis=0, concat_axis=0, tiled=True),
        lax.all_to_all(send_dy, "expert", split_axis=0, concat_axis=0, tiled=True),
        lax.all_to_all(send_gate, "expert", split_axis=0, concat_axis=0, tiled=True),
    )
    rows_x = rows_x.reshape(slot_count, feat_width)
    rows_dy = rows_dy.reshape(slot_count, feat_width)
    gate_rows = rows_gate.reshape(slot_count).astype(jnp.float32)
    up_weight = w_up[0]
    down_weight = w_down[0]
    part_hidden = jnp.dot(rows_x, up_weight, preferred_element_type=jnp.float32)
    part_query = contract(rows_dy, down_weight, 1, 1)
    full_hidden, full_query = lax.psum((part_hidden, part_query), "dp")
    act_rows, hidden_grad, score_rows = activate(full_hidden, full_query, gate_rows)
    scaled = (gate_rows[:, None] * rows_dy.astype(jnp.float32)).astype(jnp.bfloat16)
    row_grad = contract(hidden_grad, up_weight, 1, 1).astype(jnp.bfloat16)
    grad_up = contract(rows_x, hidden_grad, 0, 0).astype(jnp.bfloat16)[None]
    grad_down = contract(act_rows, scaled, 0, 0).astype(jnp.bfloat16)[None]
    back_rows, back_score = (
        lax.all_to_all(
            row_grad.reshape(experts, CAP, feat_width),
            "expert",
            split_axis=0,
            concat_axis=0,
            tiled=True,
        ),
        lax.all_to_all(
            score_rows.reshape(experts, CAP), "expert", split_axis=0, concat_axis=0, tiled=True
        ),
    )
    grad_tokens = contract(holder, back_rows.reshape(slot_count, feat_width), 1, 0).astype(
        jnp.bfloat16
    )
    grad_probs = (
        jnp.dot(flat_placed, back_score.reshape(slot_count), preferred_element_type=jnp.float32)
        .reshape(block_rows, top_count)
        .astype(jnp.bfloat16)
    )
    return (grad_tokens, grad_probs, grad_up, grad_down)


def solution(mesh):
    in_specs = (
        P("expert", "dp"),
        P("expert", "dp"),
        P("expert", None),
        P("expert", None),
        P("expert", "dp", None),
        P("expert", None, "dp"),
    )
    out_specs = (
        P("expert", "dp"),
        P("expert", None),
        P("expert", "dp", None),
        P("expert", None, "dp"),
    )
    return jax.shard_map(
        on_device, mesh=mesh, in_specs=in_specs, out_specs=out_specs, check_vma=False
    )
```

profile of v0, /device:TPU:1, one launch (start us, length us, event | category | flops | bytes accessed | tf_op | source)
XLA Modules:
  0.0 263.6 jit_solution(17180403231096362750)
XLA Ops:
  7.2 0.8 convert_reduce_fusion
  8.0 0.6 reduce-window.6
  8.6 0.2 slice_reduce_fusion
  8.9 0.8 select_reduce_fusion
  9.7 0.7 add_select_fusion
  10.4 0.1 copy.31
  10.5 1.6 fusion.5
  12.2 1.5 convolution_convert_fusion.2
  13.6 0.9 slice_bitcast_fusion.1
  14.6 38.7 %all_to_all.31 = bf16[48,8,448]{2,1,0:T(8,128)(2,1)S(1)} all-to-all(bf16[48,8,448]{2,1,0:T(8,128)(2,1)S(1)} %get-tuple-element.9), channel_id=1, replica_groups=mesh['dp'=16,'expert'=48] {'expert'}, dimensions={0} | all-to-all | bytes 688128 | tf_op jit(solution)/shard_map/all_to_all | solution.py:49
  53.2 6.1 %all-to-all-start.1 = ((bf16[48,8,448]{2,1,0:T(8,128)(2,1)}), bf16[48,8,448]{2,1,0:T(8,128)(2,1)S(1)}, u32[]{:S(2)}, u32[]{:S(2)}) async-start(bf16[48,8,448]{2,1,0:T(8,128)(2,1)} %get-tuple-element.8), calls=%async_computation.1 | async-start | bytes 786432 | tf_op jit(solution)/shard_map/all_to_all | solution.py:50
  59.4 1.7 fusion.12
  61.1 17.5 %all-to-all-done.1 = bf16[48,8,448]{2,1,0:T(8,128)(2,1)S(1)} async-done(((bf16[48,8,448]{2,1,0:T(8,128)(2,1)}), bf16[48,8,448]{2,1,0:T(8,128)(2,1)S(1)}, u32[]{:S(2)}, u32[]{:S(2)}) %all-to-all-start.1) | async-done | bytes 344096 | tf_op jit(solution)/shard_map/all_to_all | solution.py:50
  78.6 1.8 fusion.14
  80.4 0.7 copy-done.3
  81.1 0.2 copy.36
  81.2 0.9 fusion.10
  82.2 17.4 %all_to_all.32 = bf16[48,1,8]{2,1,0:T(2,128)(2,1)S(1)} all-to-all(bf16[48,1,8]{2,1,0:T(2,128)(2,1)S(1)} %all_to_all.25), channel_id=1, replica_groups=mesh['dp'=16,'expert'=48] {'expert'}, dimensions={0} | all-to-all | bytes 1536 | tf_op jit(solution)/shard_map/all_to_all | solution.py:51
  99.8 105.7 %all-reduce.3.cloned.1.call-done = (f32[384,1024]{1,0:T(8,128)}, f32[384,1024]{1,0:T(8,128)}) async-done(((f32[384,1024]{1,0:T(8,128)}, f32[384,1024]{1,0:T(8,128)}), (f32[384,1024]{1,0:T(8,128)}, f32[384,1024]{1,0:T(8,128)})) %all-reduce.3.cloned.1.call-update) | async-done | bytes 3145744 | tf_op jit(solution)/shard_map/psum | solution.py:60
  205.4 2.8 %multiply_reduce_fusion = (bf16[384]{0:T(512)(128)(2,1)S(1)}, bf16[384,1024]{1,0:T(8,128)(2,1)S(1)}) fusion(f32[384,1024]{1,0:T(8,128)} %get-tuple-element.5, f32[384,1024]{1,0:T(8,128)} %get-tuple-element.4, f32[384]{0:T(512)S(1)} %reshape.105), kind=kLoop, calls=%fused_computation.7 | loop fusion | flops 5897856 | bytes 3934464 | tf_op jit(solution)/shard_map/reduce_sum | solution.py:12
  208.2 0.7 convert_element_type.87
  208.9 13.0 %all-to-all-start.4 = ((bf16[48,1,8]{2,1,0:T(2,128)(2,1)}), bf16[48,1,8]{2,1,0:T(2,128)(2,1)S(1)}, u32[]{:S(2)}, u32[]{:S(2)}) async-start(bf16[48,1,8]{2,1,0:T(2,128)(2,1)} %convert_element_type.87), calls=%async_computation.4 | async-start | bytes 49152 | tf_op jit(solution)/shard_map/all_to_all | solution.py:74
  221.9 0.7 convolution_convert_fusion.3
  222.6 0.9 copy.33
  223.5 9.3 %all-to-all-done.4 = bf16[48,1,8]{2,1,0:T(2,128)(2,1)S(1)} async-done(((bf16[48,1,8]{2,1,0:T(2,128)(2,1)}), bf16[48,1,8]{2,1,0:T(2,128)(2,1)S(1)}, u32[]{:S(2)}, u32[]{:S(2)}) %all-to-all-start.4) | async-done | bytes 800 | tf_op jit(solution)/shard_map/all_to_all | solution.py:74
  232.8 4.7 %all-to-all-start.3 = ((bf16[48,8,448]{2,1,0:T(8,128)(2,1)}), bf16[48,8,448]{2,1,0:T(8,128)(2,1)S(1)}, u32[]{:S(2)}, u32[]{:S(2)}) async-start(bf16[48,8,448]{2,1,0:T(8,128)(2,1)} %bitcast.9), calls=%async_computation.3 | async-start | bytes 786432 | tf_op jit(solution)/shard_map/all_to_all | solution.py:67
  237.5 1.6 fusion.8
  239.1 1.8 fusion.9
  241.1 5.0 %fusion.3 = bf16[1,256,8]{2,0,1:T(2,128)(2,1)S(1)} fusion(bf16[384,1,1]{0,1,2:T(2,128)(2,1)S(1)} %reshape.108, s32[256,8]{1,0:T(8,128)S(1)} %copy.31), kind=kOutput, calls=%fused_computation.5 | convolution fusion | flops 2359296 | bytes 13056 | tf_op jit(solution)/shard_map/dot_general | solution.py:82
  246.1 0.7 copy.37
  246.8 9.0 %all-to-all-done.3 = bf16[48,8,448]{2,1,0:T(8,128)(2,1)S(1)} async-done(((bf16[48,8,448]{2,1,0:T(8,128)(2,1)}), bf16[48,8,448]{2,1,0:T(8,128)(2,1)S(1)}, u32[]{:S(2)}, u32[]{:S(2)}) %all-to-all-start.3) | async-done | bytes 344096 | tf_op jit(solution)/shard_map/all_to_all | solution.py:67
  255.7 1.0 convolution_convert_fusion.4
  (18 shorter events, 0.6 us)
Async XLA Ops:
  7.2 52.2 %copy-start = (bf16[1,448,1024]{2,1,0:T(8,128)(2,1)S(1)}, bf16[1,448,1024]{2,1,0:T(8,128)(2,1)}, u32[]{:S(2)}) copy-start(bf16[1,448,1024]{2,1,0:T(8,128)(2,1)} %param.10) | copy-start | bytes 2752516
  53.2 25.4 %all-to-all-start.1 = ((bf16[48,8,448]{2,1,0:T(8,128)(2,1)}), bf16[48,8,448]{2,1,0:T(8,128)(2,1)S(1)}, u32[]{:S(2)}, u32[]{:S(2)}) async-start(bf16[48,8,448]{2,1,0:T(8,128)(2,1)} %get-tuple-element.8), calls=%async_computation.1 | async-start | bytes 786432 | tf_op jit(solution)/shard_map/all_to_all | solution.py:50
  59.3 19.3 %copy-start.2 = (bf16[1,1024,448]{1,2,0:T(8,128)(2,1)S(1)}, bf16[1,1024,448]{1,2,0:T(8,128)(2,1)}, u32[]{:S(2)}) copy-start(bf16[1,1024,448]{1,2,0:T(8,128)(2,1)} %param.11) | copy-start | bytes 2752516
  59.3 146.1 %all-reduce.3.cloned.1.call-start = ((), (), s32[]{:S(2)}) async-start(), calls=%async_computation.5 | async-start | bytes 6291456 | tf_op jit(solution)/shard_map/psum | solution.py:60
  80.4 0.7 copy-start.3
  208.9 23.9 %all-to-all-start.4 = ((bf16[48,1,8]{2,1,0:T(2,128)(2,1)}), bf16[48,1,8]{2,1,0:T(2,128)(2,1)S(1)}, u32[]{:S(2)}, u32[]{:S(2)}) async-start(bf16[48,1,8]{2,1,0:T(2,128)(2,1)} %convert_element_type.87), calls=%async_computation.4 | async-start | bytes 49152 | tf_op jit(solution)/shard_map/all_to_all | solution.py:74
  232.8 22.9 %all-to-all-start.3 = ((bf16[48,8,448]{2,1,0:T(8,128)(2,1)}), bf16[48,8,448]{2,1,0:T(8,128)(2,1)S(1)}, u32[]{:S(2)}, u32[]{:S(2)}) async-start(bf16[48,8,448]{2,1,0:T(8,128)(2,1)} %bitcast.9), calls=%async_computation.3 | async-start | bytes 786432 | tf_op jit(solution)/shard_map/all_to_all | solution.py:67
  237.5 1.6 copy-start.1
Sparse Core Ops, SparseCore 0:
  80.5 124.8 all-reduce.2
where the time goes:
time: 268 us; the launch traced here: 264 us
  waiting for transfers between devices  141 us (53%)
  blocking collectives  56.1 us (21%)
  starting transfers between devices  23.8 us (9%)
  matrix products  15.8 us (6%)
  between operations  14.2 us (5%)
  other arithmetic  7.55 us (3%)
  local copies, waits for them, and re-layouts  4.72 us (2%)
    psum x1, waiting for transfers between devices, on_device(): full_hidden, full_query = lax.psum((part_hidden, part_query), 'dp')  106 us
    all_to_all x1, blocking collectives, on_device(): lax.all_to_all(send_x, 'expert', split_axis=0, concat_axis=0, tiled=True)  38.7 us
    all_to_all x1, waiting for transfers between devices, on_device(): lax.all_to_all(send_dy, 'expert', split_axis=0, concat_axis=0, tiled=True)  17.5 us
    all_to_all x1, blocking collectives, on_device(): lax.all_to_all(send_gate, 'expert', split_axis=0, concat_axis=0, tiled=True)  17.4 us
    all_to_all x1, starting transfers between devices, on_device(): lax.all_to_all(score_rows.reshape(experts, CAP), 'expert', split_axis=0,...  13 us
    all_to_all x1, waiting for transfers between devices, on_device(): lax.all_to_all(score_rows.reshape(experts, CAP), 'expert', split_axis=0,...  9.26 us
    dot_general x7, matrix products, contract(): lax.dot_general(left, right, (((left_dim,), (right_dim,)), ((), ())), pre...  9.15 us
    all_to_all x1, waiting for transfers between devices, on_device(): lax.all_to_all(row_grad.reshape(experts, CAP, feat_width), 'expert', spli...  8.97 us
  transfers between devices with their start and end apart: 4, of which 4 were waited for; matrix products, arithmetic and copies ran while one was open for 5% of the time, Pallas kernels for 0%

commit v1 on v0

v1 whole, which is shorter than its diff:
```python
import functools

import jax
import jax.numpy as jnp
from jax import lax
from jax.experimental import pallas as pl
from jax.experimental.pallas import tpu as pltpu
from jax.sharding import PartitionSpec as P

CAP = 8
MSG = 16
HALF = 256
STEP = 256
MESH = pl.DeviceIdType.MESH
BF16, F32 = jnp.bfloat16, jnp.float32


def dot(left, right, left_dim=1, right_dim=0):
    return lax.dot_general(
        left, right, (((left_dim,), (right_dim,)), ((), ())), preferred_element_type=F32
    )


def iota(shape, dim):
    return lax.broadcasted_iota(jnp.int32, shape, dim)


def kernel(
    experts,
    chips,
    tok_ref,
    cot_ref,
    ids_ref,
    prob_ref,
    up_hbm,
    down_hbm,
    gtok_ref,
    gprob_ref,
    gup_ref,
    gdown_ref,
    send_x,
    send_dy,
    got_x,
    got_dy,
    up,
    down,
    rows_x,
    rows_dy,
    part_h,
    part_q,
    own_h,
    own_q,
    sum_h,
    sum_q,
    hgrad,
    actg,
    score,
    ret,
    back,
    held,
    load_sem,
    send_sem,
    recv_sem,
):
    d = lax.axis_index("dp")
    g = lax.axis_index("expert")
    y, c = d // 2, lax.rem(d, 2)
    sib = 2 * y + 1 - c
    parity = lax.rem(g, 2)
    slot = lax.rem(c + parity, 2)
    block, feat = tok_ref.shape
    top = ids_ref.shape[1]
    ff = up_hbm.shape[1]
    rows = experts * CAP
    half = rows // 2
    blocks = experts // 2
    high = feat - HALF

    load_up = pltpu.make_async_copy(up_hbm, up.at[0, pl.ds(0, feat)], load_sem.at[0])
    load_down = pltpu.make_async_copy(down_hbm, down.at[0], load_sem.at[1])
    load_up.start()
    load_down.start()

    barrier = pltpu.get_barrier_semaphore()

    def greet(i, carry):
        e = lax.rem(g + i, experts)
        pl.semaphore_signal(barrier, inc=1, device_id=(d, e), device_id_type=MESH)
        pl.semaphore_signal(barrier, inc=1, device_id=(sib, e), device_id_type=MESH)
        return carry

    lax.fori_loop(1, experts, greet, 0)
    pl.semaphore_signal(barrier, inc=1, device_id=(sib, g), device_id_type=MESH)
    for i in range(1, chips):
        peer = lax.rem(y + i, chips) * 2 + c
        pl.semaphore_signal(barrier, inc=1, device_id=(peer, g), device_id_type=MESH)

    ids = ids_ref[...]
    probs = prob_ref[...].astype(F32)
    lane = iota((block, 128), 1)
    lane_hi = iota((block, HALF), 1)
    named = jnp.zeros((block, 128), F32)
    gates = jnp.zeros((block, HALF), F32)
    for k in range(top):
        column = ids[:, k : k + 1]
        named = named + jnp.where((column == lane) & (lane < experts), 1.0, 0.0)
        gates = gates + jnp.where(column == lane_hi - high, probs[:, k : k + 1], 0.0)
    named = named.astype(BF16)
    earlier = jnp.where(iota((block, block), 1) < iota((block, block), 0), 1.0, 0.0).astype(BF16)
    before = dot(earlier, named).astype(BF16)
    spread_t = jnp.where(iota((rows, 128), 0) // CAP == iota((rows, 128), 1), 1.0, 0.0).astype(BF16)
    named_t = dot(spread_t, named, 1, 1)
    before_t = dot(spread_t, before, 1, 1)
    place_t = jnp.where(
        (named_t > 0.5) & (before_t == lax.rem(iota((rows, block), 0), CAP).astype(F32)), 1.0, 0.0
    ).astype(BF16)
    spread = jnp.where(iota((128, rows), 1) // CAP == iota((128, rows), 0), 1.0, 0.0).astype(BF16)
    held[...] = jnp.where(
        (dot(named, spread) > 0.5)
        & (dot(before, spread) == lax.rem(iota((block, rows), 1), CAP).astype(F32)),
        1.0,
        0.0,
    ).astype(BF16)

    widen = jnp.where(iota((high, HALF), 0) == iota((high, HALF), 1), 1.0, 0.0).astype(BF16)

    def pack(low, hi, count):
        return jnp.concatenate(
            [low.reshape(count, CAP, HALF), hi.reshape(count, CAP, HALF)], axis=1
        ).astype(BF16)

    def unpack(message, count):
        wide = message.astype(F32)
        return (
            wide[:, :CAP].reshape(count * CAP, HALF),
            wide[:, CAP:].reshape(count * CAP, HALF),
        )

    tok_hi = (dot(tok_ref[:, HALF:], widen) + gates).astype(BF16)
    send_x[...] = pack(dot(place_t, tok_ref[:, :HALF]), dot(place_t, tok_hi), experts)
    cot_hi = dot(cot_ref[:, HALF:], widen).astype(BF16)
    send_dy[...] = pack(dot(place_t, cot_ref[:, :HALF]), dot(place_t, cot_hi), experts)
    for s in range(2):
        up[s, feat:, :] = jnp.zeros((2 * HALF - feat, ff), BF16)

    pl.semaphore_wait(barrier, 2 * experts - 1 + chips - 1)

    def dispatch(source, target, n):
        def remote(e, core):
            return pltpu.make_async_remote_copy(
                src_ref=source.at[e],
                dst_ref=target.at[slot, g // 2],
                send_sem=send_sem.at[n],
                recv_sem=recv_sem.at[n],
                device_id=(core, e),
                device_id_type=MESH,
            )

        def body(i, carry):
            remote(lax.rem(g + i, experts), 2 * y + parity).start()
            return carry

        lax.fori_loop(1, experts, body, 0)

        @pl.when(c == parity)
        def _():
            pltpu.make_async_copy(source.at[g], target.at[0, g // 2], recv_sem.at[n]).start()

        @pl.when(c != parity)
        def _():
            remote(g, sib).start()

    def to_sibling(source, target, n):
        copy = pltpu.make_async_remote_copy(
            src_ref=source,
            dst_ref=target,
            send_sem=send_sem.at[n],
            recv_sem=recv_sem.at[n],
            device_id=(sib, g),
            device_id_type=MESH,
        )
        copy.start()
        return copy

    def arrived(buffer, n):
        pltpu.make_async_copy(buffer, buffer, recv_sem.at[n]).wait()

    def sent(buffer, n):
        pltpu.make_async_copy(buffer, buffer, send_sem.at[n]).wait()

    dispatch(send_x, got_x, 0)
    load_up.wait()
    load_down.wait()
    up_copy = to_sibling(up.at[0, pl.ds(0, feat)], up.at[1, pl.ds(0, feat)], 2)
    down_copy = to_sibling(down.at[0], down.at[1], 3)
    dispatch(send_dy, got_dy, 1)

    turns = [chips // 2]
    for i in range(1, (chips + 1) // 2):
        turns += [i, chips - i]

    def to_peers(source_of, target, n):
        for i in turns:
            peer = lax.rem(y + i, chips)
            pltpu.make_async_remote_copy(
                src_ref=source_of(peer),
                dst_ref=target,
                send_sem=send_sem.at[n],
                recv_sem=recv_sem.at[n],
                device_id=(peer * 2 + c, g),
                device_id_type=MESH,
            ).start()

    unit = ff // chips

    arrived(got_x, 0)
    low, hi = unpack(got_x[0], blocks)
    gate = jnp.sum(jnp.where(iota((half, HALF), 1) == g + high, hi, 0.0), axis=1, keepdims=True)
    rows_x[0] = jnp.concatenate([low, hi], axis=1).astype(BF16)
    low, hi = unpack(got_x[1], blocks)
    rows_x[2] = jnp.concatenate([low, hi], axis=1).astype(BF16)
    up_copy.wait()
    for n in range(ff // STEP):
        cols = pl.ds(n * STEP, STEP)
        product = dot(rows_x[0], up[0, :, cols]) + dot(rows_x[2], up[1, :, cols])
        for m in range(STEP // unit):
            piece = product[:, m * unit : (m + 1) * unit]
            own_h[n * (STEP // unit) + m] = piece
            part_h[n * (STEP // unit) + m] = piece.astype(BF16)
    to_peers(lambda peer: part_h.at[peer], sum_h.at[y], 4)
    x_copy = to_sibling(rows_x.at[2], rows_x.at[1], 5)

    arrived(got_dy, 1)
    for s in range(2):
        low, hi = unpack(got_dy[s], blocks)
        rows_dy[2 * s] = jnp.concatenate([low, hi], axis=1).astype(BF16)
    down_copy.wait()
    for n in range(ff // STEP):
        part = pl.ds(n * STEP, STEP)
        product = dot(rows_dy[0, :, :feat], down[0, part, :], 1, 1) + dot(
            rows_dy[2, :, :feat], down[1, part, :], 1, 1
        )
        for m in range(STEP // unit):
            piece = product[:, m * unit : (m + 1) * unit]
            own_q[n * (STEP // unit) + m] = piece
            part_q[n * (STEP // unit) + m] = piece.astype(BF16)
    to_peers(lambda peer: part_q.at[peer], sum_q.at[y], 6)
    dy_copy = to_sibling(rows_dy.at[2], rows_dy.at[1], 7)

    arrived(sum_h.at[pl.ds(0, chips - 1)], 4)
    hidden = own_h[y]
    for i in range(1, chips):
        hidden = hidden + sum_h[lax.rem(y + i, chips)].astype(F32)
    sigma = jax.nn.sigmoid(hidden)
    act = (hidden * sigma).astype(BF16).astype(F32)
    slope = gate * (sigma * (1.0 + hidden * (1.0 - sigma)))
    arrived(sum_q.at[pl.ds(0, chips - 1)], 6)
    query = own_q[y]
    for i in range(1, chips):
        query = query + sum_q[lax.rem(y + i, chips)].astype(F32)
    hgrad[0, y] = (slope * query).astype(BF16)
    to_peers(lambda peer: hgrad.at[0, y], hgrad.at[0, y], 8)
    score[y] = lax.dot_general(
        jnp.ones((8, unit), F32),
        act * query,
        (((1,), (1,)), ((), ())),
        precision=lax.Precision.HIGHEST,
        preferred_element_type=F32,
    )
    to_peers(lambda peer: score.at[y], score.at[y], 9)
    actg[0, y] = (gate * act).astype(BF16)
    to_peers(lambda peer: actg.at[0, y], actg.at[0, y], 10)

    arrived(hgrad.at[0, pl.ds(0, chips - 1)], 8)
    hgrad_copy = to_sibling(hgrad.at[0], hgrad.at[1], 11)
    arrived(score.at[pl.ds(0, chips - 1)], 9)
    total = score[0]
    for i in range(1, chips):
        total = total + score[i]
    mark = jnp.where(
        (iota((8, HALF), 0) == 0) & (iota((8, HALF), 1) == g + high), 1.0, 0.0
    ).astype(BF16)
    score_lane = dot(total.astype(BF16), mark, 0, 0)
    grad_rows = jnp.concatenate([hgrad[0, i] for i in range(chips)], axis=1)
    for s in range(2):
        low = dot(grad_rows, up[s, :HALF, :], 1, 1)
        hi = dot(grad_rows, up[s, HALF:, :], 1, 1) + score_lane
        ret[s] = pack(low, hi, blocks)

    def remote_back(s, j, core, b):
        return pltpu.make_async_remote_copy(
            src_ref=ret.at[s, j],
            dst_ref=back.at[g],
            send_sem=send_sem.at[12],
            recv_sem=recv_sem.at[12],
            device_id=(core, b),
            device_id_type=MESH,
        )

    def body(i, carry):
        j = lax.rem(g // 2 + i, blocks)
        b = 2 * j + c
        remote_back(0, j, d, b).start()
        remote_back(1, j, sib, b).start()
        return carry

    lax.fori_loop(1, blocks, body, 0)
    first = 2 * (g // 2) + c
    remote_back(1, g // 2, sib, first).start()

    @pl.when(c == parity)
    def _():
        pltpu.make_async_copy(ret.at[0, g // 2], back.at[g], recv_sem.at[12]).start()

    @pl.when(c != parity)
    def _():
        remote_back(0, g // 2, d, first).start()

    x_copy.wait()
    hgrad_copy.wait()
    own_x = jnp.concatenate([rows_x[0], rows_x[1]], axis=0)
    for n in range(ff // STEP):
        units = range(n * (STEP // unit), (n + 1) * (STEP // unit))
        right = jnp.concatenate(
            [jnp.concatenate([hgrad[0, i], hgrad[1, i]], axis=0) for i in units], axis=1
        )
        gup_ref[:, pl.ds(n * STEP, STEP)] = dot(own_x, right, 0, 0)[:feat].astype(BF16)
    arrived(actg.at[0, pl.ds(0, chips - 1)], 10)
    actg_copy = to_sibling(actg.at[0], actg.at[1], 13)
    dy_copy.wait()
    own_dy = jnp.concatenate([rows_dy[0], rows_dy[1]], axis=0)
    actg_copy.wait()
    for n in range(ff // STEP):
        units = range(n * (STEP // unit), (n + 1) * (STEP // unit))
        left = jnp.concatenate(
            [jnp.concatenate([actg[0, i], actg[1, i]], axis=0) for i in units], axis=1
        )
        gdown_ref[pl.ds(n * STEP, STEP), :] = dot(left, own_dy, 0, 0)[:, :feat].astype(BF16)

    arrived(back, 12)
    low, hi = unpack(back[...], experts)
    gtok_ref[:, :HALF] = dot(held[...], low.astype(BF16)).astype(BF16)
    top_lanes = dot(held[...], hi.astype(BF16))
    gtok_ref[:, HALF:] = top_lanes[:, :high].astype(BF16)
    found = jnp.zeros((block, top), F32)
    for k in range(top):
        value = jnp.sum(
            jnp.where((ids[:, k : k + 1] == lane_hi - high) & (lane_hi >= high), top_lanes, 0.0),
            axis=1,
            keepdims=True,
        )
        found = found + jnp.where(iota((block, top), 1) == k, value, 0.0)
    gprob_ref[...] = found.astype(BF16)

    for n, buffer in ((0, send_x), (1, send_dy), (12, back)):

        @pl.when(c == parity)
        def _(n=n, buffer=buffer):
            sent(buffer.at[pl.ds(0, experts - 1)], n)

        @pl.when(c != parity)
        def _(n=n, buffer=buffer):
            sent(buffer, n)

    for n, buffer in ((4, sum_h), (6, sum_q), (8, hgrad.at[0]), (9, score), (10, actg.at[0])):
        sent(buffer.at[pl.ds(0, chips - 1)], n)


def on_device(tokens, cotangent, expert_ids, route_probs, w_up, w_down):
    experts = lax.axis_size("expert")
    chips = lax.axis_size("dp") // 2
    block, feat = tokens.shape
    top = expert_ids.shape[1]
    ff = w_up.shape[2]
    half = experts * CAP // 2
    blocks = experts // 2
    unit = ff // chips
    wide = 2 * HALF
    vmem = pl.BlockSpec(memory_space=pltpu.VMEM)
    anywhere = pl.BlockSpec(memory_space=pl.ANY)
    grad_tokens, grad_probs, grad_up, grad_down = pl.pallas_call(
        functools.partial(kernel, experts, chips),
        out_shape=(
            jax.ShapeDtypeStruct((block, feat), BF16),
            jax.ShapeDtypeStruct((block, top), BF16),
            jax.ShapeDtypeStruct((feat, ff), BF16),
            jax.ShapeDtypeStruct((ff, feat), BF16),
        ),
        in_specs=[vmem] * 4 + [anywhere] * 2,
        out_specs=[vmem] * 4,
        scratch_shapes=[
            pltpu.VMEM((experts, MSG, HALF), BF16),
            pltpu.VMEM((experts, MSG, HALF), BF16),
            pltpu.VMEM((2, blocks, MSG, HALF), BF16),
            pltpu.VMEM((2, blocks, MSG, HALF), BF16),
            pltpu.VMEM((2, wide, ff), BF16),
            pltpu.VMEM((2, ff, feat), BF16),
            pltpu.VMEM((3, half, wide), BF16),
            pltpu.VMEM((3, half, wide), BF16),
            pltpu.VMEM((chips, half, unit), BF16),
            pltpu.VMEM((chips, half, unit), BF16),
            pltpu.VMEM((chips, half, unit), F32),
            pltpu.VMEM((chips, half, unit), F32),
            pltpu.VMEM((chips, half, unit), BF16),
            pltpu.VMEM((chips, half, unit), BF16),
            pltpu.VMEM((2, chips, half, unit), BF16),
            pltpu.VMEM((2, chips, half, unit), BF16),
            pltpu.VMEM((chips, 8, half), F32),
            pltpu.VMEM((2, blocks, MSG, HALF), BF16),
            pltpu.VMEM((experts, MSG, HALF), BF16),
            pltpu.VMEM((block, experts * CAP), BF16),
            pltpu.SemaphoreType.DMA((2,)),
            pltpu.SemaphoreType.DMA((14,)),
            pltpu.SemaphoreType.DMA((14,)),
        ],
        compiler_params=pltpu.CompilerParams(
            collective_id=0, has_side_effects=True, vmem_limit_bytes=56 * 2**20
        ),
        name="expert_backward",
    )(tokens, cotangent, expert_ids, route_probs, w_up[0], w_down[0])
    return (grad_tokens, grad_probs, grad_up[None], grad_down[None])


def solution(mesh):
    in_specs = (
        P("expert", "dp"),
        P("expert", "dp"),
        P("expert", None),
        P("expert", None),
        P("expert", "dp", None),
        P("expert", None, "dp"),
    )
    out_specs = (
        P("expert", "dp"),
        P("expert", None),
        P("expert", "dp", None),
        P("expert", None, "dp"),
    )
    return jax.shard_map(
        on_device, mesh=mesh, in_specs=in_specs, out_specs=out_specs, check_vma=False
    )
```

time: 268 us -> 110 us (0.41); the launches traced: 264 us -> 109 us
  waiting for transfers between devices: 141 us -> 0 us
  Pallas kernels: 0 us -> 95.2 us
  blocking collectives: 56.1 us -> 0 us
  starting transfers between devices: 23.8 us -> 0 us
  matrix products: 15.8 us -> 0 us
  between operations: 14.2 us -> 0.66 us
  local copies, waits for them, and re-layouts: 4.72 us -> 13.5 us
  other arithmetic: 7.55 us -> 0 us
    psum x1 -> x0, waiting for transfers between devices: 106 us -> none  [on_device(): full_hidden, full_query = lax.psum((part_hidden, part_query), 'dp')]
    pallas_call x0 -> x1, Pallas kernels: none -> 95.2 us  [on_device(): pl.pallas_call(functools.partial(kernel, experts, chips), out_shape=(jax....]
    all_to_all x2 -> x0, blocking collectives: 56.1 us -> none  [the longest x1 38.7 us: on_device(): lax.all_to_all(send_x, 'expert', split_axis=0, concat_axis=0, tiled=True)]
    all_to_all x3 -> x0, waiting for transfers between devices: 35.8 us -> none  [the longest x1 17.5 us: on_device(): lax.all_to_all(send_dy, 'expert', split_axis=0, concat_axis=0, tiled=True)]
    all_to_all x3 -> x0, starting transfers between devices: 23.8 us -> none  [the longest x1 13 us: on_device(): lax.all_to_all(score_rows.reshape(experts, CAP), 'expert', split_axis=0,...]
    dot_general x9 -> x0, matrix products: 15.8 us -> none  [the longest x7 9.15 us: contract(): lax.dot_general(left, right, (((left_dim,), (right_dim,)), ((), ())), pre...]
    unnamed x9 -> x15, local copies, waits for them, and re-layouts: 0.83 us -> 13.5 us
    reduce_sum x4 -> x0, other arithmetic: 5.97 us -> none  [the longest x1 2.77 us: activate(): jnp.sum(act_rows.astype(jnp.float32) * query, axis=1).astype(jnp.bfloat16)]
  transfers between devices with their start and end apart: 4 -> 0, of which waited for: 4 -> 0; matrix products, arithmetic and copies ran while one was open for 5% -> 0% of each run, Pallas kernels for 0% -> 0%
where the time goes in v1:
time: 110 us; the launch traced here: 109 us
  Pallas kernels  95.2 us (87%)
  local copies, waits for them, and re-layouts  13.5 us (12%)
    pallas_call x1, Pallas kernels, on_device(): pl.pallas_call(functools.partial(kernel, experts, chips), out_shape=(jax....  95.2 us
    unnamed x15, local copies, waits for them, and re-layouts  13.5 us

profile of v1, /device:TPU:1, one launch (start us, length us, event | category | flops | bytes accessed | tf_op | source)
XLA Modules:
  0.0 109.4 jit_solution(11517844514259731549)
XLA Ops:
  0.6 0.0 copy-start.1
  0.6 1.5 %copy.14.prob_ref = bf16[256,8]{1,0:T(8,128)(2,1)} copy(bf16[256,8]{0,1:T(8,128)(2,1)} %param.9) | data formatting | bytes 8192 | tf_op args[3]
  2.1 1.5 %copy.13.ids_ref = s32[256,8]{1,0:T(8,128)} copy(s32[256,8]{0,1:T(8,128)} %param.8) | data formatting | bytes 16384 | tf_op args[2]
  3.6 1.8 %copy.11.tok_ref = bf16[256,448]{1,0:T(8,128)(2,1)} copy(bf16[256,448]{0,1:T(8,128)(2,1)} %param.6) | data formatting | bytes 458752 | tf_op args[0]
  5.4 1.8 %copy.12.cot_ref = bf16[256,448]{1,0:T(8,128)(2,1)} copy(bf16[256,448]{0,1:T(8,128)(2,1)} %param.7) | data formatting | bytes 458752 | tf_op args[1]
  7.2 0.0 copy-done.1
  7.2 1.3 %copy.10 = bf16[1,1024,448]{2,1,0:T(8,128)(2,1)} copy(bf16[1,1024,448]{1,2,0:T(8,128)(2,1)S(1)} %copy-done.1) | data formatting | bytes 1835008 | tf_op args[5]
  8.5 95.2 %expert_backward.1 = (bf16[256,448]{1,0:T(8,128)(2,1)}, bf16[256,8]{1,0:T(8,128)(2,1)}, bf16[448,1024]{1,0:T(8,128)(2,1)}, bf16[1024,448]{1,0:T(8,128)(2,1)}) custom-call(bf16[256,448]{1,0:T(8,128)(2,1)} %copy.11.tok_ref, bf16[256,448]{1,0:T(8,128)(2,1)} %copy.12.cot_ref, s32[256,8]{1,0:T(8,128)} %copy.13.ids_ref, bf16[256,8]{1,0:T(8,128)(2,1)} %copy.14.prob_ref, ...), custom_call_target="tpu_custom_call" | custom-call | tf_op jit(solution)/shard_map/expert_backward/pallas_call | solution.py:381
  103.7 0.0 copy-start.2
  103.7 1.8 %copy.15 = bf16[256,448]{0,1:T(8,128)(2,1)} copy(bf16[256,448]{1,0:T(8,128)(2,1)} %get-tuple-element.12) | data formatting | bytes 458752
  105.5 0.0 copy-done.2
  105.5 0.7 copy.16
  106.2 0.0 copy-start
  106.2 2.3 %copy.17 = bf16[1,1024,448]{1,2,0:T(8,128)(2,1)} copy(bf16[1,1024,448]{2,1,0:T(8,128)(2,1)} %bitcast.5) | data formatting | bytes 1835008
  108.5 0.0 copy-done
  108.5 0.9 copy.19
Async XLA Ops:
  0.6 6.5 %copy-start.1 = (bf16[1,1024,448]{1,2,0:T(8,128)(2,1)S(1)}, bf16[1,1024,448]{1,2,0:T(8,128)(2,1)}, u32[]{:S(2)}) copy-start(bf16[1,1024,448]{1,2,0:T(8,128)(2,1)} %param.11) | copy-start | bytes 2752516
  103.7 1.8 %copy-start.2 = (bf16[256,8]{1,0:T(8,128)(2,1)S(1)}, bf16[256,8]{1,0:T(8,128)(2,1)}, u32[]{:S(2)}) copy-start(bf16[256,8]{1,0:T(8,128)(2,1)} %get-tuple-element.13) | copy-start | bytes 12292
  106.2 2.3 %copy-start = (bf16[448,1024]{1,0:T(8,128)(2,1)S(1)}, bf16[448,1024]{1,0:T(8,128)(2,1)}, u32[]{:S(2)}) copy-start(bf16[448,1024]{1,0:T(8,128)(2,1)} %get-tuple-element.10) | copy-start | bytes 2752516

commit v2 on v1

v2 whole, which is shorter than its diff:
```python
import functools

import jax
import jax.numpy as jnp
from jax import lax
from jax.experimental import pallas as pl
from jax.experimental.pallas import tpu as pltpu
from jax.sharding import PartitionSpec as P

CAP = 8
MSG = 16
HALF = 256
STEP = 256
ROW = 4
MESH = pl.DeviceIdType.MESH
BF16, F32 = jnp.bfloat16, jnp.float32


def dot(left, right, left_dim=1, right_dim=0):
    return lax.dot_general(
        left, right, (((left_dim,), (right_dim,)), ((), ())), preferred_element_type=F32
    )


def iota(shape, dim):
    return lax.broadcasted_iota(jnp.int32, shape, dim)


def kernel(
    experts,
    chips,
    tok_hbm,
    cot_hbm,
    ids_hbm,
    prob_hbm,
    up_hbm,
    down_hbm,
    gtok_ref,
    gprob_ref,
    gup_ref,
    gdown_ref,
    tok_ref,
    cot_ref,
    ids_ref,
    prob_ref,
    send_x,
    send_dy,
    got_x,
    got_dy,
    up,
    down,
    rows_x,
    rows_dy,
    part_h,
    part_q,
    own_h,
    own_q,
    sum_h,
    sum_q,
    hgrad,
    actg,
    score,
    ret,
    back,
    held,
    load_sem,
    send_sem,
    recv_sem,
):
    d = lax.axis_index("dp")
    g = lax.axis_index("expert")
    y, c = d // 2, lax.rem(d, 2)
    sib = 2 * y + 1 - c
    parity = lax.rem(g, 2)
    slot = lax.rem(c + parity, 2)
    feat, block = tok_hbm.shape
    top = ids_hbm.shape[0]
    ff = up_hbm.shape[1]
    rows = experts * CAP
    half = rows // 2
    blocks = experts // 2
    high = feat - HALF
    rings = experts // ROW
    z, x = g // ROW, lax.rem(g, ROW)
    part = half // 2
    place_of_mine = (x // 2) * rings + z

    def far_first(i):
        j = rings - 1 - i
        near = (j + 1) // 2
        return lax.rem(z + jnp.where(lax.rem(j, 2) == 1, near, rings - near), rings)

    loads = [
        pltpu.make_async_copy(source, target, load_sem.at[n])
        for n, (source, target) in enumerate(
            (
                (ids_hbm, ids_ref),
                (prob_hbm, prob_ref),
                (tok_hbm, tok_ref),
                (cot_hbm, cot_ref),
                (up_hbm, up.at[0, pl.ds(0, feat)]),
                (down_hbm, down.at[0, pl.ds(0, feat)]),
            )
        )
    ]
    for load in loads:
        load.start()

    barrier = pltpu.get_barrier_semaphore()

    def greet(i, carry):
        e = lax.rem(g + i, experts)
        pl.semaphore_signal(barrier, inc=1, device_id=(d, e), device_id_type=MESH)
        pl.semaphore_signal(barrier, inc=1, device_id=(sib, e), device_id_type=MESH)
        return carry

    lax.fori_loop(1, experts, greet, 0)
    pl.semaphore_signal(barrier, inc=1, device_id=(sib, g), device_id_type=MESH)
    for i in range(1, chips):
        peer = lax.rem(y + i, chips) * 2 + c
        pl.semaphore_signal(barrier, inc=1, device_id=(peer, g), device_id_type=MESH)

    loads[0].wait()
    loads[1].wait()
    ids = ids_ref[...]
    probs = prob_ref[...].astype(F32)
    number = iota((128, block), 0)
    number_hi = iota((2 * HALF - feat, block), 0)
    named = jnp.zeros((128, block), F32)
    gates = jnp.zeros((2 * HALF - feat, block), F32)
    for k in range(top):
        line = ids[k : k + 1, :]
        named = named + jnp.where((line == number) & (number < experts), 1.0, 0.0)
        gates = gates + jnp.where(line == number_hi, probs[k : k + 1, :], 0.0)
    named = named.astype(BF16)
    earlier = jnp.where(iota((block, block), 0) < iota((block, block), 1), 1.0, 0.0).astype(BF16)
    before = dot(named, earlier).astype(BF16)
    spread = jnp.where(iota((rows, 128), 0) // CAP == iota((rows, 128), 1), 1.0, 0.0).astype(BF16)
    place = jnp.where(
        (dot(spread, named) > 0.5)
        & (dot(spread, before) == lax.rem(iota((rows, block), 0), CAP).astype(F32)),
        1.0,
        0.0,
    ).astype(BF16)
    held[...] = place

    def pack(low, hi, count):
        return jnp.concatenate(
            [low.reshape(count, CAP, HALF), hi.reshape(count, CAP, HALF)], axis=1
        ).astype(BF16)

    def unpack(message, count):
        wide = message.astype(F32)
        return (
            wide[:, :CAP].reshape(count * CAP, HALF),
            wide[:, CAP:].reshape(count * CAP, HALF),
        )

    loads[2].wait()
    tok_hi = jnp.concatenate([tok_ref[HALF:, :], gates.astype(BF16)], axis=0)
    send_x[...] = pack(dot(place, tok_ref[:HALF, :], 1, 1), dot(place, tok_hi, 1, 1), experts)
    loads[3].wait()
    cot_hi = jnp.concatenate([cot_ref[HALF:, :], jnp.zeros(gates.shape, BF16)], axis=0)
    send_dy[...] = pack(dot(place, cot_ref[:HALF, :], 1, 1), dot(place, cot_hi, 1, 1), experts)
    for s in range(2):
        up[s, feat:, :] = jnp.zeros((2 * HALF - feat, ff), BF16)
        down[s, feat:, :] = jnp.zeros((2 * HALF - feat, ff), BF16)

    pl.semaphore_wait(barrier, 2 * experts - 1 + chips - 1)

    def dispatch(source, target, n):
        def remote(e, core):
            return pltpu.make_async_remote_copy(
                src_ref=source.at[e],
                dst_ref=target.at[slot, place_of_mine],
                send_sem=send_sem.at[n],
                recv_sem=recv_sem.at[n],
                device_id=(core, e),
                device_id_type=MESH,
            )

        def body(i, carry):
            first = far_first(i) * ROW
            for turn in range(ROW):
                remote(first + lax.rem(x + turn, ROW), 2 * y + parity).start()
            return carry

        lax.fori_loop(0, rings - 1, body, 0)
        for turn in range(1, ROW):
            remote(z * ROW + lax.rem(x + turn, ROW), 2 * y + parity).start()

        @pl.when(c == parity)
        def _():
            pltpu.make_async_copy(source.at[g], target.at[0, place_of_mine], recv_sem.at[n]).start()

        @pl.when(c != parity)
        def _():
            remote(g, sib).start()

    def to_sibling(source, target, n):
        copy = pltpu.make_async_remote_copy(
            src_ref=source,
            dst_ref=target,
            send_sem=send_sem.at[n],
            recv_sem=recv_sem.at[n],
            device_id=(sib, g),
            device_id_type=MESH,
        )
        copy.start()
        return copy

    def arrived(buffer, n):
        pltpu.make_async_copy(buffer, buffer, recv_sem.at[n]).wait()

    def sent(buffer, n):
        pltpu.make_async_copy(buffer, buffer, send_sem.at[n]).wait()

    dispatch(send_x, got_x, 0)
    loads[4].wait()
    loads[5].wait()
    up_copy = to_sibling(up.at[0, pl.ds(0, feat)], up.at[1, pl.ds(0, feat)], 2)
    down_copy = to_sibling(down.at[0, pl.ds(0, feat)], down.at[1, pl.ds(0, feat)], 3)
    dispatch(send_dy, got_dy, 1)

    turns = [chips // 2]
    for i in range(1, (chips + 1) // 2):
        turns += [i, chips - i]

    def to_peers(source_of, target, n):
        for i in turns:
            peer = lax.rem(y + i, chips)
            pltpu.make_async_remote_copy(
                src_ref=source_of(peer),
                dst_ref=target,
                send_sem=send_sem.at[n],
                recv_sem=recv_sem.at[n],
                device_id=(peer * 2 + c, g),
                device_id_type=MESH,
            ).start()

    unit = ff // chips

    arrived(got_x, 0)
    low, hi = unpack(got_x[0], blocks)
    gate = jnp.sum(jnp.where(iota((half, HALF), 1) == g + high, hi, 0.0), axis=1, keepdims=True)
    rows_x[0] = jnp.concatenate([low, hi], axis=1).astype(BF16)
    low, hi = unpack(got_x[1], blocks)
    rows_x[2] = jnp.concatenate([low, hi], axis=1).astype(BF16)
    up_copy.wait()
    for n in range(ff // STEP):
        cols = pl.ds(n * STEP, STEP)
        product = dot(rows_x[0], up[0, :, cols]) + dot(rows_x[2], up[1, :, cols])
        for m in range(STEP // unit):
            piece = product[:, m * unit : (m + 1) * unit]
            own_h[n * (STEP // unit) + m] = piece
            part_h[n * (STEP // unit) + m] = piece.astype(BF16)
    to_peers(lambda peer: part_h.at[peer], sum_h.at[y], 4)
    x_copy = to_sibling(rows_x.at[2], rows_x.at[1], 5)

    arrived(got_dy, 1)
    for s in range(2):
        low, hi = unpack(got_dy[s], blocks)
        rows_dy[2 * s] = jnp.concatenate([low, hi], axis=1).astype(BF16)
    down_copy.wait()
    for n in range(ff // STEP):
        cols = pl.ds(n * STEP, STEP)
        product = dot(rows_dy[0], down[0, :, cols]) + dot(rows_dy[2], down[1, :, cols])
        for m in range(STEP // unit):
            piece = product[:, m * unit : (m + 1) * unit]
            own_q[n * (STEP // unit) + m] = piece
            part_q[n * (STEP // unit) + m] = piece.astype(BF16)
    to_peers(lambda peer: part_q.at[peer], sum_q.at[y], 6)
    dy_copy = to_sibling(rows_dy.at[2], rows_dy.at[1], 7)

    arrived(sum_h.at[pl.ds(0, chips - 1)], 4)
    hidden = own_h[y]
    for i in range(1, chips):
        hidden = hidden + sum_h[lax.rem(y + i, chips)].astype(F32)
    sigma = jax.nn.sigmoid(hidden)
    act = (hidden * sigma).astype(BF16).astype(F32)
    slope = gate * (sigma * (1.0 + hidden * (1.0 - sigma)))
    actg[0, y] = (gate * act).astype(BF16)
    arrived(sum_q.at[pl.ds(0, chips - 1)], 6)
    for p in range(2):
        span = pl.ds(p * part, part)
        query = own_q[y, span]
        for i in range(1, chips):
            query = query + sum_q[lax.rem(y + i, chips), span].astype(F32)
        here = slice(p * part, (p + 1) * part)
        hgrad[0, y, span] = (slope[here] * query).astype(BF16)
        to_peers(lambda peer: hgrad.at[0, y, span], hgrad.at[0, y, span], 8 + 6 * p)
        score[p, y] = lax.dot_general(
            jnp.ones((8, unit), F32),
            act[here] * query,
            (((1,), (1,)), ((), ())),
            precision=lax.Precision.HIGHEST,
            preferred_element_type=F32,
        )
        to_peers(lambda peer: score.at[p, y], score.at[p, y], 9 + 6 * p)

    mark = jnp.where(
        (iota((8, HALF), 0) == 0) & (iota((8, HALF), 1) == g + high), 1.0, 0.0
    ).astype(BF16)

    def remote_back(s, j, core, b):
        return pltpu.make_async_remote_copy(
            src_ref=ret.at[s, j],
            dst_ref=back.at[g],
            send_sem=send_sem.at[12],
            recv_sem=recv_sem.at[12],
            device_id=(core, b),
            device_id_type=MESH,
        )

    for p in range(2):
        span = pl.ds(p * part, part)
        arrived(hgrad.at[0, pl.ds(0, chips - 1), span], 8 + 6 * p)
        arrived(score.at[p, pl.ds(0, chips - 1)], 9 + 6 * p)
        total = score[p, 0]
        for i in range(1, chips):
            total = total + score[p, i]
        score_lane = dot(total.astype(BF16), mark, 0, 0)
        grad_rows = jnp.concatenate([hgrad[0, i, span] for i in range(chips)], axis=1)
        for s in range(2):
            low = dot(grad_rows, up[s, :HALF, :], 1, 1)
            hi = dot(grad_rows, up[s, HALF:, :], 1, 1) + score_lane
            ret[s, pl.ds(p * rings, rings)] = pack(low, hi, rings)
        column = 2 * p + c

        def body(i, carry, p=p, column=column):
            other = far_first(i)
            for s, core in ((0, d), (1, sib)):
                remote_back(s, p * rings + other, core, other * ROW + column).start()
            return carry

        lax.fori_loop(0, rings - 1, body, 0)
        remote_back(1, p * rings + z, sib, z * ROW + column).start()

        @pl.when(x == column)
        def _(p=p):
            pltpu.make_async_copy(ret.at[0, p * rings + z], back.at[g], recv_sem.at[12]).start()

        @pl.when(x != column)
        def _(p=p, column=column):
            remote_back(0, p * rings + z, d, z * ROW + column).start()

    hgrad_copy = to_sibling(hgrad.at[0], hgrad.at[1], 11)
    to_peers(lambda peer: actg.at[0, y], actg.at[0, y], 10)

    x_copy.wait()
    hgrad_copy.wait()
    own_x = jnp.concatenate([rows_x[0], rows_x[1]], axis=0)
    for n in range(ff // STEP):
        units = range(n * (STEP // unit), (n + 1) * (STEP // unit))
        right = jnp.concatenate(
            [jnp.concatenate([hgrad[0, i], hgrad[1, i]], axis=0) for i in units], axis=1
        )
        gup_ref[:, pl.ds(n * STEP, STEP)] = dot(own_x, right, 0, 0)[:feat].astype(BF16)
    arrived(actg.at[0, pl.ds(0, chips - 1)], 10)
    actg_copy = to_sibling(actg.at[0], actg.at[1], 13)
    dy_copy.wait()
    own_dy = jnp.concatenate([rows_dy[0], rows_dy[1]], axis=0)
    actg_copy.wait()
    for n in range(ff // STEP):
        units = range(n * (STEP // unit), (n + 1) * (STEP // unit))
        right = jnp.concatenate(
            [jnp.concatenate([actg[0, i], actg[1, i]], axis=0) for i in units], axis=1
        )
        gdown_ref[:, pl.ds(n * STEP, STEP)] = dot(own_dy, right, 0, 0)[:feat].astype(BF16)

    arrived(back, 12)
    low, hi = unpack(back[...], experts)
    gtok_ref[:HALF, :] = dot(low.astype(BF16), held[...], 0, 0).astype(BF16)
    summed = dot(hi.astype(BF16), held[...], 0, 0)
    gtok_ref[HALF:, :] = summed[:high].astype(BF16)
    found = jnp.zeros((top, block), F32)
    for k in range(top):
        value = jnp.sum(
            jnp.where(ids[k : k + 1, :] == number_hi, summed[high:], 0.0), axis=0, keepdims=True
        )
        found = found + jnp.where(iota((top, block), 0) == k, value, 0.0)
    gprob_ref[...] = found.astype(BF16)

    for n, buffer in ((0, send_x), (1, send_dy), (12, back)):

        @pl.when(c == parity)
        def _(n=n, buffer=buffer):
            sent(buffer.at[pl.ds(0, experts - 1)], n)

        @pl.when(c != parity)
        def _(n=n, buffer=buffer):
            sent(buffer, n)

    for n, buffer in ((4, sum_h), (6, sum_q), (10, actg.at[0])):
        sent(buffer.at[pl.ds(0, chips - 1)], n)
    for p in range(2):
        sent(hgrad.at[0, pl.ds(0, chips - 1), pl.ds(p * part, part)], 8 + 6 * p)
        sent(score.at[p, pl.ds(0, chips - 1)], 9 + 6 * p)


def hand_over(*refs):
    count = len(refs) // 2
    sem = refs[-1]
    copies = [pltpu.make_async_copy(refs[n], refs[count + n], sem.at[n]) for n in range(count)]
    for copy in copies:
        copy.start()
    for copy in copies:
        copy.wait()


def on_device(tokens, cotangent, expert_ids, route_probs, w_up, w_down):
    experts = lax.axis_size("expert")
    chips = lax.axis_size("dp") // 2
    block, feat = tokens.shape
    top = expert_ids.shape[1]
    ff = w_up.shape[2]
    half = experts * CAP // 2
    blocks = experts // 2
    unit = ff // chips
    wide = 2 * HALF
    vmem = pl.BlockSpec(memory_space=pltpu.VMEM)
    anywhere = pl.BlockSpec(memory_space=pl.ANY)
    results = pl.pallas_call(
        functools.partial(kernel, experts, chips),
        out_shape=(
            jax.ShapeDtypeStruct((feat, block), BF16),
            jax.ShapeDtypeStruct((top, block), BF16),
            jax.ShapeDtypeStruct((feat, ff), BF16),
            jax.ShapeDtypeStruct((feat, ff), BF16),
        ),
        in_specs=[anywhere] * 6,
        out_specs=[vmem] * 4,
        scratch_shapes=[
            pltpu.VMEM((feat, block), BF16),
            pltpu.VMEM((feat, block), BF16),
            pltpu.VMEM((top, block), jnp.int32),
            pltpu.VMEM((top, block), BF16),
            pltpu.VMEM((experts, MSG, HALF), BF16),
            pltpu.VMEM((experts, MSG, HALF), BF16),
            pltpu.VMEM((2, blocks, MSG, HALF), BF16),
            pltpu.VMEM((2, blocks, MSG, HALF), BF16),
            pltpu.VMEM((2, wide, ff), BF16),
            pltpu.VMEM((2, wide, ff), BF16),
            pltpu.VMEM((3, half, wide), BF16),
            pltpu.VMEM((3, half, wide), BF16),
            pltpu.VMEM((chips, half, unit), BF16),
            pltpu.VMEM((chips, half, unit), BF16),
            pltpu.VMEM((chips, half, unit), F32),
            pltpu.VMEM((chips, half, unit), F32),
            pltpu.VMEM((chips, half, unit), BF16),
            pltpu.VMEM((chips, half, unit), BF16),
            pltpu.VMEM((2, chips, half, unit), BF16),
            pltpu.VMEM((2, chips, half, unit), BF16),
            pltpu.VMEM((2, chips, 8, half // 2), F32),
            pltpu.VMEM((2, blocks, MSG, HALF), BF16),
            pltpu.VMEM((experts, MSG, HALF), BF16),
            pltpu.VMEM((experts * CAP, block), BF16),
            pltpu.SemaphoreType.DMA((6,)),
            pltpu.SemaphoreType.DMA((16,)),
            pltpu.SemaphoreType.DMA((16,)),
        ],
        compiler_params=pltpu.CompilerParams(
            collective_id=0, has_side_effects=True, vmem_limit_bytes=56 * 2**20
        ),
        name="expert_backward",
    )(tokens.T, cotangent.T, expert_ids.T, route_probs.T, w_up[0], w_down[0].T)
    grad_tokens, grad_probs, grad_up, grad_down = pl.pallas_call(
        hand_over,
        out_shape=tuple(jax.ShapeDtypeStruct(r.shape, r.dtype) for r in results),
        in_specs=[anywhere] * 4,
        out_specs=[anywhere] * 4,
        scratch_shapes=[pltpu.SemaphoreType.DMA((4,))],
        name="hand_over",
    )(*results)
    return (grad_tokens.T, grad_probs.T, grad_up[None], grad_down.T[None])


def solution(mesh):
    in_specs = (
        P("expert", "dp"),
        P("expert", "dp"),
        P("expert", None),
        P("expert", None),
        P("expert", "dp", None),
        P("expert", None, "dp"),
    )
    out_specs = (
        P("expert", "dp"),
        P("expert", None),
        P("expert", "dp", None),
        P("expert", None, "dp"),
    )
    return jax.shard_map(
        on_device, mesh=mesh, in_specs=in_specs, out_specs=out_specs, check_vma=False
    )
```

time: 110 us -> 155 us (1.41)
  Pallas kernels: 95.2 us -> 154 us
  local copies, waits for them, and re-layouts: 13.5 us -> 0 us
    pallas_call x0 -> x1, Pallas kernels: none -> 63.8 us  [on_device(): pl.pallas_call(hand_over, out_shape=tuple((jax.ShapeDtypeStruct(r.shape,...]
    unnamed x15 -> x0, local copies, waits for them, and re-layouts: 13.5 us -> none
    pallas_call x1, Pallas kernels: 95.2 us -> 90.4 us  [on_device(): pl.pallas_call(functools.partial(kernel, experts, chips), out_shape=(jax....]
where the time goes in v2:
time: 155 us
  Pallas kernels  154 us (99%)
    pallas_call x1, Pallas kernels, on_device(): pl.pallas_call(functools.partial(kernel, experts, chips), out_shape=(jax....  90.4 us
    pallas_call x1, Pallas kernels, on_device(): pl.pallas_call(hand_over, out_shape=tuple((jax.ShapeDtypeStruct(r.shape,...  63.8 us

profile of v2, /device:TPU:1, one launch (start us, length us, event | category | flops | bytes accessed | tf_op | source)
XLA Modules:
  0.0 154.9 jit_solution(16365495751981336129)
XLA Ops:
  0.6 90.4 %expert_backward.1 = (bf16[448,256]{1,0:T(8,128)(2,1)}, bf16[8,256]{1,0:T(8,128)(2,1)}, bf16[448,1024]{1,0:T(8,128)(2,1)}, bf16[448,1024]{1,0:T(8,128)(2,1)}) custom-call(bf16[448,256]{1,0:T(8,128)(2,1)} %bitcast.16, bf16[448,256]{1,0:T(8,128)(2,1)} %bitcast.17, s32[8,256]{1,0:T(8,128)} %bitcast.18, bf16[8,256]{1,0:T(8,128)(2,1)} %bitcast.19, ...), custom_call_target="tpu_custom_call" | custom-call | tf_op jit(solution)/shard_map/expert_backward/pallas_call | solution.py:423
  91.1 63.8 %hand_over.1 = (bf16[448,256]{1,0:T(8,128)(2,1)}, bf16[8,256]{1,0:T(8,128)(2,1)}, bf16[448,1024]{1,0:T(8,128)(2,1)}, bf16[448,1024]{1,0:T(8,128)(2,1)}) custom-call(bf16[448,256]{1,0:T(8,128)(2,1)} %get-tuple-element.12.refs_0_, bf16[8,256]{1,0:T(8,128)(2,1)} %get-tuple-element.13.refs_1_, bf16[448,1024]{1,0:T(8,128)(2,1)} %get-tuple-element.14.refs_2_, ...), custom_call_target="tpu_custom_call" | custom-call | tf_op jit(solution)/shard_map/hand_over/pallas_call | solution.py:467

commit v3 on v2

--- a/solution.py
+++ b/solution.py
@@ -37,8 +37,8 @@
     down_hbm,
     gtok_ref,
     gprob_ref,
-    gup_ref,
-    gdown_ref,
+    gup_hbm,
+    gdown_hbm,
     tok_ref,
     cot_ref,
     ids_ref,
@@ -63,6 +63,8 @@
     ret,
     back,
     held,
+    gup_ref,
+    gdown_ref,
     load_sem,
     send_sem,
     recv_sem,
@@ -356,6 +358,8 @@
             [jnp.concatenate([hgrad[0, i], hgrad[1, i]], axis=0) for i in units], axis=1
         )
         gup_ref[:, pl.ds(n * STEP, STEP)] = dot(own_x, right, 0, 0)[:feat].astype(BF16)
+    gup_copy = pltpu.make_async_copy(gup_ref, gup_hbm, load_sem.at[6])
+    gup_copy.start()
     arrived(actg.at[0, pl.ds(0, chips - 1)], 10)
     actg_copy = to_sibling(actg.at[0], actg.at[1], 13)
     dy_copy.wait()
@@ -368,6 +372,9 @@
         )
         gdown_ref[:, pl.ds(n * STEP, STEP)] = dot(own_dy, right, 0, 0)[:feat].astype(BF16)
 
+    gdown_copy = pltpu.make_async_copy(gdown_ref, gdown_hbm, load_sem.at[7])
+    gdown_copy.start()
+
     arrived(back, 12)
     low, hi = unpack(back[...], experts)
     gtok_ref[:HALF, :] = dot(low.astype(BF16), held[...], 0, 0).astype(BF16)
@@ -381,6 +388,8 @@
         found = found + jnp.where(iota((top, block), 0) == k, value, 0.0)
     gprob_ref[...] = found.astype(BF16)
 
+    gup_copy.wait()
+    gdown_copy.wait()
     for n, buffer in ((0, send_x), (1, send_dy), (12, back)):
 
         @pl.when(c == parity)
@@ -399,13 +408,18 @@
 
 
 def hand_over(*refs):
-    count = len(refs) // 2
+    count = len(refs) // 3
+    source, target, middle = refs[:count], refs[count : 2 * count], refs[2 * count : 3 * count]
     sem = refs[-1]
-    copies = [pltpu.make_async_copy(refs[n], refs[count + n], sem.at[n]) for n in range(count)]
-    for copy in copies:
-        copy.start()
-    for copy in copies:
-        copy.wait()
+    loads = [pltpu.make_async_copy(source[n], middle[n], sem.at[0, n]) for n in range(count)]
+    stores = [pltpu.make_async_copy(middle[n], target[n], sem.at[1, n]) for n in range(count)]
+    for load in loads:
+        load.start()
+    for load, store in zip(loads, stores):
+        load.wait()
+        store.start()
+    for store in stores:
+        store.wait()
 
 
 def on_device(tokens, cotangent, expert_ids, route_probs, w_up, w_down):
@@ -429,7 +443,7 @@
             jax.ShapeDtypeStruct((feat, ff), BF16),
         ),
         in_specs=[anywhere] * 6,
-        out_specs=[vmem] * 4,
+        out_specs=[vmem] * 2 + [anywhere] * 2,
         scratch_shapes=[
             pltpu.VMEM((feat, block), BF16),
             pltpu.VMEM((feat, block), BF16),
@@ -455,7 +469,9 @@
             pltpu.VMEM((2, blocks, MSG, HALF), BF16),
             pltpu.VMEM((experts, MSG, HALF), BF16),
             pltpu.VMEM((experts * CAP, block), BF16),
-            pltpu.SemaphoreType.DMA((6,)),
+            pltpu.VMEM((feat, ff), BF16),
+            pltpu.VMEM((feat, ff), BF16),
+            pltpu.SemaphoreType.DMA((8,)),
             pltpu.SemaphoreType.DMA((16,)),
             pltpu.SemaphoreType.DMA((16,)),
         ],
@@ -469,7 +485,7 @@
         out_shape=tuple(jax.ShapeDtypeStruct(r.shape, r.dtype) for r in results),
         in_specs=[anywhere] * 4,
         out_specs=[anywhere] * 4,
-        scratch_shapes=[pltpu.SemaphoreType.DMA((4,))],
+        scratch_shapes=[pltpu.VMEM(r.shape, r.dtype) for r in results] + [pltpu.SemaphoreType.DMA((2, 4))],
         name="hand_over",
     )(*results)
     return (grad_tokens.T, grad_probs.T, grad_up[None], grad_down.T[None])

time: 155 us -> 93.7 us (0.60)
  Pallas kernels: 154 us -> 92.9 us
    pallas_call x1, Pallas kernels: 63.8 us -> 2.61 us  [on_device(): pl.pallas_call(hand_over, out_shape=tuple((jax.ShapeDtypeStruct(r.shape,...]
where the time goes in v3:
time: 93.7 us; the launch traced here: 93.6 us
  Pallas kernels  92.9 us (99%)
    pallas_call x1, Pallas kernels, on_device(): pl.pallas_call(functools.partial(kernel, experts, chips), out_shape=(jax....  90.3 us
    pallas_call x1, Pallas kernels, on_device(): pl.pallas_call(hand_over, out_shape=tuple((jax.ShapeDtypeStruct(r.shape,...  2.61 us

profile of v3, /device:TPU:1, one launch (start us, length us, event | category | flops | bytes accessed | tf_op | source)
XLA Modules:
  0.0 93.6 jit_solution(11092629184796820275)
XLA Ops:
  0.6 90.3 %expert_backward.1 = (bf16[448,256]{1,0:T(8,128)(2,1)}, bf16[8,256]{1,0:T(8,128)(2,1)}, bf16[448,1024]{1,0:T(8,128)(2,1)}, bf16[448,1024]{1,0:T(8,128)(2,1)}) custom-call(bf16[448,256]{1,0:T(8,128)(2,1)} %bitcast.16, bf16[448,256]{1,0:T(8,128)(2,1)} %bitcast.17, s32[8,256]{1,0:T(8,128)} %bitcast.18, bf16[8,256]{1,0:T(8,128)(2,1)} %bitcast.19, ...), custom_call_target="tpu_custom_call" | custom-call | tf_op jit(solution)/shard_map/expert_backward/pallas_call | solution.py:437
  91.0 2.6 %hand_over.1 = (bf16[448,256]{1,0:T(8,128)(2,1)}, bf16[8,256]{1,0:T(8,128)(2,1)}, bf16[448,1024]{1,0:T(8,128)(2,1)}, bf16[448,1024]{1,0:T(8,128)(2,1)}) custom-call(bf16[448,256]{1,0:T(8,128)(2,1)} %get-tuple-element.12.refs_0_, bf16[8,256]{1,0:T(8,128)(2,1)} %get-tuple-element.13.refs_1_, bf16[448,1024]{1,0:T(8,128)(2,1)} %get-tuple-element.14.refs_2_, ...), custom_call_target="tpu_custom_call" | custom-call | tf_op jit(solution)/shard_map/hand_over/pallas_call | solution.py:483

commit v4 on v3

v4 whole, which is shorter than its diff:
```python
import functools

import jax
import jax.numpy as jnp
from jax import lax
from jax.experimental import pallas as pl
from jax.experimental.pallas import tpu as pltpu
from jax.sharding import PartitionSpec as P

CAP = 8
PARTS = 2
SUB = CAP // PARTS
FIELDS = 4
MSG = FIELDS * SUB
HALF = 256
QUARTER = 128
STEP = 256
ROW = 4
MESH = pl.DeviceIdType.MESH
BF16, F32 = jnp.bfloat16, jnp.float32


def dot(left, right, left_dim=1, right_dim=0):
    return lax.dot_general(
        left, right, (((left_dim,), (right_dim,)), ((), ())), preferred_element_type=F32
    )


def iota(shape, dim):
    return lax.broadcasted_iota(jnp.int32, shape, dim)


def kernel(
    experts,
    chips,
    tok_hbm,
    cot_hbm,
    ids_hbm,
    prob_hbm,
    up_hbm,
    down_hbm,
    gtok_ref,
    gprob_ref,
    gup_hbm,
    gdown_hbm,
    tok_ref,
    cot_ref,
    ids_ref,
    prob_ref,
    send,
    got,
    up,
    down,
    rows_x,
    rows_dy,
    part,
    own,
    sums,
    hgrad,
    actg,
    score,
    ret,
    back,
    placed,
    combined,
    gup_ref,
    gdown_ref,
    load_sem,
    send_sem,
    recv_sem,
):
    d = lax.axis_index("dp")
    g = lax.axis_index("expert")
    y, c = d // 2, lax.rem(d, 2)
    sib = 2 * y + 1 - c
    parity = lax.rem(g, 2)
    slot = lax.rem(c + parity, 2)
    feat, block = tok_hbm.shape
    top = ids_hbm.shape[0]
    ff = up_hbm.shape[1]
    blocks = experts // 2
    count = blocks * SUB
    high = feat - HALF
    rings = experts // ROW
    z, x = g // ROW, lax.rem(g, ROW)

    def far_first(i):
        j = rings - 1 - i
        near = (j + 1) // 2
        return lax.rem(z + jnp.where(lax.rem(j, 2) == 1, near, rings - near), rings)

    loads = [
        pltpu.make_async_copy(source, target, load_sem.at[n])
        for n, (source, target) in enumerate(
            (
                (ids_hbm, ids_ref),
                (prob_hbm, prob_ref),
                (tok_hbm, tok_ref),
                (cot_hbm, cot_ref),
                (up_hbm, up.at[0, pl.ds(0, feat)]),
                (down_hbm, down.at[0, pl.ds(0, feat)]),
            )
        )
    ]
    for load in loads:
        load.start()

    barrier = pltpu.get_barrier_semaphore()

    def greet(i, carry):
        e = lax.rem(g + i, experts)
        pl.semaphore_signal(barrier, inc=1, device_id=(d, e), device_id_type=MESH)
        pl.semaphore_signal(barrier, inc=1, device_id=(sib, e), device_id_type=MESH)
        return carry

    lax.fori_loop(1, experts, greet, 0)
    pl.semaphore_signal(barrier, inc=1, device_id=(sib, g), device_id_type=MESH)
    for i in range(1, chips):
        peer = lax.rem(y + i, chips) * 2 + c
        pl.semaphore_signal(barrier, inc=1, device_id=(peer, g), device_id_type=MESH)

    loads[0].wait()
    loads[1].wait()
    ids = ids_ref[...]
    probs = prob_ref[...].astype(F32)
    number = iota((128, block), 0)
    number_hi = iota((2 * HALF - feat, block), 0)
    named = jnp.zeros((128, block), F32)
    gates = jnp.zeros((2 * HALF - feat, block), F32)
    for k in range(top):
        line = ids[k : k + 1, :]
        named = named + jnp.where((line == number) & (number < experts), 1.0, 0.0)
        gates = gates + jnp.where(line == number_hi, probs[k : k + 1, :], 0.0)
    named = named.astype(BF16)
    earlier = jnp.where(iota((block, block), 0) < iota((block, block), 1), 1.0, 0.0).astype(BF16)
    before = dot(named, earlier).astype(BF16)
    lines = experts * MSG
    spread = jnp.where(iota((lines, 128), 0) // MSG == iota((lines, 128), 1), 1.0, 0.0).astype(BF16)
    named_line = dot(spread, named)
    rank_line = dot(spread, before)
    rank = lax.rem(iota((lines, block), 0), SUB)
    field = lax.rem(iota((lines, block), 0) // SUB, FIELDS)
    for k in range(PARTS):
        fills = (named_line > 0.5) & (rank_line == (rank + k * SUB).astype(F32))
        for q in range(FIELDS):
            placed[k, :, q * block : (q + 1) * block] = jnp.where(
                fills & (field == q), 1.0, 0.0
            ).astype(BF16)

    loads[2].wait()
    loads[3].wait()
    source = jnp.concatenate(
        [
            tok_ref[:HALF, :],
            jnp.concatenate([tok_ref[HALF:, :], gates.astype(BF16)], axis=0),
            cot_ref[:HALF, :],
            jnp.concatenate([cot_ref[HALF:, :], jnp.zeros(gates.shape, BF16)], axis=0),
        ],
        axis=1,
    )

    def fill(k):
        send[k] = dot(placed[k], source, 1, 1).astype(BF16).reshape(experts, MSG, HALF)

    fill(0)
    for s in range(2):
        up[s, feat:, :] = jnp.zeros((2 * HALF - feat, ff), BF16)
        down[s, feat:, :] = jnp.zeros((2 * HALF - feat, ff), BF16)

    pl.semaphore_wait(barrier, 2 * experts - 1 + chips - 1)

    def dispatch(n):
        def remote(e, core):
            return pltpu.make_async_remote_copy(
                src_ref=send.at[n, e],
                dst_ref=got.at[n, slot, g // 2],
                send_sem=send_sem.at[n],
                recv_sem=recv_sem.at[n],
                device_id=(core, e),
                device_id_type=MESH,
            )

        def body(i, carry):
            first = far_first(i) * ROW
            for turn in range(ROW):
                remote(first + lax.rem(x + turn, ROW), 2 * y + parity).start()
            return carry

        lax.fori_loop(0, rings - 1, body, 0)
        for turn in range(1, ROW):
            remote(z * ROW + lax.rem(x + turn, ROW), 2 * y + parity).start()

        @pl.when(c == parity)
        def _():
            pltpu.make_async_copy(send.at[n, g], got.at[n, 0, g // 2], recv_sem.at[n]).start()

        @pl.when(c != parity)
        def _():
            remote(g, sib).start()

    def to_sibling(source, target, n):
        copy = pltpu.make_async_remote_copy(
            src_ref=source,
            dst_ref=target,
            send_sem=send_sem.at[n],
            recv_sem=recv_sem.at[n],
            device_id=(sib, g),
            device_id_type=MESH,
        )
        copy.start()
        return copy

    def arrived(buffer, n):
        pltpu.make_async_copy(buffer, buffer, recv_sem.at[n]).wait()

    def sent(buffer, n):
        pltpu.make_async_copy(buffer, buffer, send_sem.at[n]).wait()

    dispatch(0)
    loads[4].wait()
    loads[5].wait()
    up_copy = to_sibling(up.at[0, pl.ds(0, feat)], up.at[1, pl.ds(0, feat)], 2)
    down_copy = to_sibling(down.at[0, pl.ds(0, feat)], down.at[1, pl.ds(0, feat)], 3)
    fill(1)
    dispatch(1)

    turns = [chips // 2]
    for i in range(1, (chips + 1) // 2):
        turns += [i, chips - i]

    def to_peers(source_of, target, n):
        for i in turns:
            peer = lax.rem(y + i, chips)
            pltpu.make_async_remote_copy(
                src_ref=source_of(peer),
                dst_ref=target,
                send_sem=send_sem.at[n],
                recv_sem=recv_sem.at[n],
                device_id=(peer * 2 + c, g),
                device_id_type=MESH,
            ).start()

    unit = ff // chips

    i = iota((count, blocks * MSG), 0)
    line = (i // SUB) * MSG + lax.rem(i, SUB) - iota((count, blocks * MSG), 1)
    take = jnp.concatenate(
        [jnp.where(line == -q * SUB, 1.0, 0.0).astype(BF16) for q in range(FIELDS)], axis=0
    )

    def received(k):
        arrived(got.at[k], k)
        for s in range(2):
            fields = dot(take, got[k, s].reshape(blocks * MSG, HALF))
            low, hi, dlow, dhi = (fields[q * count : (q + 1) * count] for q in range(FIELDS))
            rows_x[k, 2 * s] = jnp.concatenate([low, hi], axis=1).astype(BF16)
            rows_dy[k, 2 * s] = jnp.concatenate([dlow, dhi], axis=1).astype(BF16)
            if s == 0:
                lane = iota((count, HALF), 1)
                gate = jnp.sum(jnp.where(lane == g + high, hi, 0.0), axis=1, keepdims=True)
        if k == 0:
            up_copy.wait()
            down_copy.wait()
        for n in range(ff // STEP):
            cols = pl.ds(n * STEP, STEP)
            product = jnp.concatenate(
                [
                    dot(rows_x[k, 0], up[0, :, cols]) + dot(rows_x[k, 2], up[1, :, cols]),
                    dot(rows_dy[k, 0], down[0, :, cols]) + dot(rows_dy[k, 2], down[1, :, cols]),
                ],
                axis=0,
            )
            for m in range(STEP // unit):
                piece = product[:, m * unit : (m + 1) * unit]
                own[k, n * (STEP // unit) + m] = piece
                part[k, n * (STEP // unit) + m] = piece.astype(BF16)
        to_peers(lambda peer: part.at[k, peer], sums.at[k, y], 4 + k)
        x_copy = to_sibling(rows_x.at[k, 2], rows_x.at[k, 1], 12 + k)
        dy_copy = to_sibling(rows_dy.at[k, 2], rows_dy.at[k, 1], 14 + k)
        return gate, x_copy, dy_copy

    def activate(k, gate):
        arrived(sums.at[k, pl.ds(0, chips - 1)], 4 + k)
        total = own[k, y]
        for i in range(1, chips):
            total = total + sums[k, lax.rem(y + i, chips)].astype(F32)
        hidden, query = total[:count], total[count:]
        sigma = jax.nn.sigmoid(hidden)
        hgrad[k, 0, y] = (gate * query * (sigma * (1.0 + hidden * (1.0 - sigma)))).astype(BF16)
        to_peers(lambda peer: hgrad.at[k, 0, y], hgrad.at[k, 0, y], 6 + k)
        act = (hidden * sigma).astype(BF16).astype(F32)
        score[k, y] = lax.dot_general(
            jnp.ones((8, unit), F32),
            act * query,
            (((1,), (1,)), ((), ())),
            precision=lax.Precision.HIGHEST,
            preferred_element_type=F32,
        )
        to_peers(lambda peer: score.at[k, y], score.at[k, y], 8 + k)
        actg[k, 0, y] = (gate * act).astype(BF16)

    def share_act(k):
        to_peers(lambda peer: actg.at[k, 0, y], actg.at[k, 0, y], 10 + k)

    def send_back(k):
        arrived(hgrad.at[k, 0, pl.ds(0, chips - 1)], 6 + k)
        hgrad_copy = to_sibling(hgrad.at[k, 0], hgrad.at[k, 1], 16 + k)
        arrived(score.at[k, pl.ds(0, chips - 1)], 8 + k)
        total = score[k, 0]
        for i in range(1, chips):
            total = total + score[k, i]
        mark = jnp.where(
            (iota((8, HALF), 0) == 0) & (iota((8, HALF), 1) == g + high), 1.0, 0.0
        ).astype(BF16)
        score_lane = dot(total.astype(BF16), mark, 0, 0)
        grad_rows = jnp.concatenate([hgrad[k, 0, i] for i in range(chips)], axis=1)
        for s in range(2):
            low = dot(grad_rows, up[s, :HALF, :], 1, 1).astype(BF16)
            hi = (dot(grad_rows, up[s, HALF:, :], 1, 1) + score_lane).astype(BF16)
            stack = jnp.concatenate(
                [low[:, :QUARTER], low[:, QUARTER:], hi[:, :QUARTER], hi[:, QUARTER:]], axis=0
            )
            ret[k, s] = dot(take, stack, 0, 0).astype(BF16).reshape(blocks, MSG, QUARTER)

        def remote_back(s, core, b):
            return pltpu.make_async_remote_copy(
                src_ref=ret.at[k, s, b // 2],
                dst_ref=back.at[k, g],
                send_sem=send_sem.at[20 + k],
                recv_sem=recv_sem.at[20 + k],
                device_id=(core, b),
                device_id_type=MESH,
            )

        def body(i, carry):
            first = far_first(i) * ROW + c
            for b in (first, first + 2):
                remote_back(0, d, b).start()
                remote_back(1, sib, b).start()
            return carry

        lax.fori_loop(0, rings - 1, body, 0)
        first = z * ROW + c
        other = z * ROW + lax.rem(x + 2, ROW)
        beside = z * ROW + lax.rem(x + 1, ROW)
        across = z * ROW + lax.rem(x + 3, ROW)

        @pl.when(c == parity)
        def _():
            remote_back(0, d, other).start()
            remote_back(1, sib, other).start()
            remote_back(1, sib, g).start()
            pltpu.make_async_copy(ret.at[k, 0, g // 2], back.at[k, g], recv_sem.at[20 + k]).start()

        @pl.when(c != parity)
        def _():
            for b in (beside, across):
                remote_back(0, d, b).start()
                remote_back(1, sib, b).start()

        return hgrad_copy

    def combine(k):
        arrived(back.at[k], 20 + k)
        lines_back = back[k].reshape(experts * MSG, QUARTER)
        for q in range(FIELDS):
            term = dot(lines_back, placed[k, :, q * block : (q + 1) * block], 0, 0)
            combined[q] = term if k == 0 else combined[q] + term

    gate_0, x_copy_0, dy_copy_0 = received(0)
    gate_1, x_copy_1, dy_copy_1 = received(1)
    activate(0, gate_0)
    activate(1, gate_1)
    share_act(0)
    share_act(1)
    hgrad_copy_0 = send_back(0)
    hgrad_copy_1 = send_back(1)

    def weight_grad(rows, factor, target):
        left = jnp.concatenate([rows[k, i] for k in range(PARTS) for i in range(2)], axis=0)
        for n in range(ff // STEP):
            units = range(n * (STEP // unit), (n + 1) * (STEP // unit))
            right = jnp.concatenate(
                [
                    jnp.concatenate(
                        [factor[k, i, u] for k in range(PARTS) for i in range(2)], axis=0
                    )
                    for u in units
                ],
                axis=1,
            )
            target[:, pl.ds(n * STEP, STEP)] = dot(left, right, 0, 0)[:feat].astype(BF16)

    for copy in (x_copy_0, x_copy_1, hgrad_copy_0, hgrad_copy_1):
        copy.wait()
    weight_grad(rows_x, hgrad, gup_ref)
    gup_copy = pltpu.make_async_copy(gup_ref, gup_hbm, load_sem.at[6])
    gup_copy.start()
    actg_copies = []
    for k in range(PARTS):
        arrived(actg.at[k, 0, pl.ds(0, chips - 1)], 10 + k)
        actg_copies.append(to_sibling(actg.at[k, 0], actg.at[k, 1], 18 + k))
    combine(0)
    for copy in (dy_copy_0, dy_copy_1, *actg_copies):
        copy.wait()
    weight_grad(rows_dy, actg, gdown_ref)
    gdown_copy = pltpu.make_async_copy(gdown_ref, gdown_hbm, load_sem.at[7])
    gdown_copy.start()

    combine(1)
    for q in range(FIELDS - 1):
        gtok_ref[q * QUARTER : (q + 1) * QUARTER, :] = combined[q].astype(BF16)
    rest = feat - (FIELDS - 1) * QUARTER
    gtok_ref[(FIELDS - 1) * QUARTER :, :] = combined[FIELDS - 1, :rest].astype(BF16)
    summed = combined[FIELDS - 1, rest:]
    found = jnp.zeros((top, block), F32)
    for k in range(top):
        value = jnp.sum(
            jnp.where(ids[k : k + 1, :] == number_hi, summed, 0.0), axis=0, keepdims=True
        )
        found = found + jnp.where(iota((top, block), 0) == k, value, 0.0)
    gprob_ref[...] = found.astype(BF16)

    gup_copy.wait()
    gdown_copy.wait()
    for k in range(PARTS):
        for n, buffer in ((k, send), (20 + k, back)):

            @pl.when(c == parity)
            def _(n=n, buffer=buffer, k=k):
                sent(buffer.at[k, pl.ds(0, experts - 1)], n)

            @pl.when(c != parity)
            def _(n=n, buffer=buffer, k=k):
                sent(buffer.at[k], n)

        for n, buffer in ((4, sums.at[k]), (6, hgrad.at[k, 0]), (8, score.at[k]), (10, actg.at[k, 0])):
            sent(buffer.at[pl.ds(0, chips - 1)], n + k)


def hand_over(*refs):
    count = len(refs) // 3
    source, target, middle = refs[:count], refs[count : 2 * count], refs[2 * count : 3 * count]
    sem = refs[-1]
    loads = [pltpu.make_async_copy(source[n], middle[n], sem.at[0, n]) for n in range(count)]
    stores = [pltpu.make_async_copy(middle[n], target[n], sem.at[1, n]) for n in range(count)]
    for load in loads:
        load.start()
    for load, store in zip(loads, stores):
        load.wait()
        store.start()
    for store in stores:
        store.wait()


def on_device(tokens, cotangent, expert_ids, route_probs, w_up, w_down):
    experts = lax.axis_size("expert")
    chips = lax.axis_size("dp") // 2
    block, feat = tokens.shape
    top = expert_ids.shape[1]
    ff = w_up.shape[2]
    blocks = experts // 2
    count = blocks * SUB
    unit = ff // chips
    wide = 2 * HALF
    vmem = pl.BlockSpec(memory_space=pltpu.VMEM)
    anywhere = pl.BlockSpec(memory_space=pl.ANY)
    results = pl.pallas_call(
        functools.partial(kernel, experts, chips),
        out_shape=(
            jax.ShapeDtypeStruct((feat, block), BF16),
            jax.ShapeDtypeStruct((top, block), BF16),
            jax.ShapeDtypeStruct((feat, ff), BF16),
            jax.ShapeDtypeStruct((feat, ff), BF16),
        ),
        in_specs=[anywhere] * 6,
        out_specs=[vmem] * 2 + [anywhere] * 2,
        scratch_shapes=[
            pltpu.VMEM((feat, block), BF16),
            pltpu.VMEM((feat, block), BF16),
            pltpu.VMEM((top, block), jnp.int32),
            pltpu.VMEM((top, block), BF16),
            pltpu.VMEM((PARTS, experts, MSG, HALF), BF16),
            pltpu.VMEM((PARTS, 2, blocks, MSG, HALF), BF16),
            pltpu.VMEM((2, wide, ff), BF16),
            pltpu.VMEM((2, wide, ff), BF16),
            pltpu.VMEM((PARTS, 3, count, wide), BF16),
            pltpu.VMEM((PARTS, 3, count, wide), BF16),
            pltpu.VMEM((PARTS, chips, 2 * count, unit), BF16),
            pltpu.VMEM((PARTS, chips, 2 * count, unit), F32),
            pltpu.VMEM((PARTS, chips, 2 * count, unit), BF16),
            pltpu.VMEM((PARTS, 2, chips, count, unit), BF16),
            pltpu.VMEM((PARTS, 2, chips, count, unit), BF16),
            pltpu.VMEM((PARTS, chips, 8, count), F32),
            pltpu.VMEM((PARTS, 2, blocks, MSG, QUARTER), BF16),
            pltpu.VMEM((PARTS, experts, MSG, QUARTER), BF16),
            pltpu.VMEM((PARTS, experts * MSG, FIELDS * block), BF16),
            pltpu.VMEM((FIELDS, QUARTER, block), F32),
            pltpu.VMEM((feat, ff), BF16),
            pltpu.VMEM((feat, ff), BF16),
            pltpu.SemaphoreType.DMA((8,)),
            pltpu.SemaphoreType.DMA((22,)),
            pltpu.SemaphoreType.DMA((22,)),
        ],
        compiler_params=pltpu.CompilerParams(
            collective_id=0, has_side_effects=True, vmem_limit_bytes=56 * 2**20
        ),
        name="expert_backward",
    )(tokens.T, cotangent.T, expert_ids.T, route_probs.T, w_up[0], w_down[0].T)
    grad_tokens, grad_probs, grad_up, grad_down = pl.pallas_call(
        hand_over,
        out_shape=tuple(jax.ShapeDtypeStruct(r.shape, r.dtype) for r in results),
        in_specs=[anywhere] * 4,
        out_specs=[anywhere] * 4,
        scratch_shapes=[pltpu.VMEM(r.shape, r.dtype) for r in results] + [pltpu.SemaphoreType.DMA((2, 4))],
        name="hand_over",
    )(*results)
    return (grad_tokens.T, grad_probs.T, grad_up[None], grad_down.T[None])


def solution(mesh):
    in_specs = (
        P("expert", "dp"),
        P("expert", "dp"),
        P("expert", None),
        P("expert", None),
        P("expert", "dp", None),
        P("expert", None, "dp"),
    )
    out_specs = (
        P("expert", "dp"),
        P("expert", None),
        P("expert", "dp", None),
        P("expert", None, "dp"),
    )
    return jax.shard_map(
        on_device, mesh=mesh, in_specs=in_specs, out_specs=out_specs, check_vma=False
    )
```

time: 93.7 us -> 90.7 us (0.968)
  Pallas kernels: 92.9 us -> 89.9 us
    pallas_call x1, Pallas kernels: 90.3 us -> 87.3 us  [on_device(): pl.pallas_call(functools.partial(kernel, experts, chips), out_shape=(jax....]
where the time goes in v4:
time: 90.7 us; the launch traced here: 90.5 us
  Pallas kernels  89.9 us (99%)
    pallas_call x1, Pallas kernels, on_device(): pl.pallas_call(functools.partial(kernel, experts, chips), out_shape=(jax....  87.3 us
    pallas_call x1, Pallas kernels, on_device(): pl.pallas_call(hand_over, out_shape=tuple((jax.ShapeDtypeStruct(r.shape,...  2.61 us

profile of v4, /device:TPU:1, one launch (start us, length us, event | category | flops | bytes accessed | tf_op | source)
XLA Modules:
  0.0 90.5 jit_solution(10895827474154413953)
XLA Ops:
  0.6 87.3 %expert_backward.1 = (bf16[448,256]{1,0:T(8,128)(2,1)}, bf16[8,256]{1,0:T(8,128)(2,1)}, bf16[448,1024]{1,0:T(8,128)(2,1)}, bf16[448,1024]{1,0:T(8,128)(2,1)}) custom-call(bf16[448,256]{1,0:T(8,128)(2,1)} %bitcast.16, bf16[448,256]{1,0:T(8,128)(2,1)} %bitcast.17, s32[8,256]{1,0:T(8,128)} %bitcast.18, bf16[8,256]{1,0:T(8,128)(2,1)} %bitcast.19, ...), custom_call_target="tpu_custom_call" | custom-call | tf_op jit(solution)/shard_map/expert_backward/pallas_call | solution.py:468
  87.9 2.6 %hand_over.1 = (bf16[448,256]{1,0:T(8,128)(2,1)}, bf16[8,256]{1,0:T(8,128)(2,1)}, bf16[448,1024]{1,0:T(8,128)(2,1)}, bf16[448,1024]{1,0:T(8,128)(2,1)}) custom-call(bf16[448,256]{1,0:T(8,128)(2,1)} %get-tuple-element.12.refs_0_, bf16[8,256]{1,0:T(8,128)(2,1)} %get-tuple-element.13.refs_1_, bf16[448,1024]{1,0:T(8,128)(2,1)} %get-tuple-element.14.refs_2_, ...), custom_call_target="tpu_custom_call" | custom-call | tf_op jit(solution)/shard_map/hand_over/pallas_call | solution.py:510
